TPU v7x, 32 devices: a whole 2x2x4 slice. The times are simulated.
32 devices in a mesh: pipe: 8 (over y, x, core), dp: 4 (over z).
Axes of the slice: x: 2, y: 2, z: 4, core: 2. Of those that a mesh axis runs over, the one named last changes fastest.
Arguments:
- x_saved: bfloat16 [8, 1024, 1024], P('pipe', 'dp'), may hold values from -6 to 6
- up_weights: bfloat16 [8, 1024, 2048], P('pipe', 'dp'), may hold values from -0.1875 to 0.1875
- down_weights: bfloat16 [8, 2048, 1024], P('pipe', 'dp'), may hold values from -0.125 to 0.125
- norm_gain: float32 [8, 1024], P('pipe'), may hold values from 0.1 to 1.9
- layer_scale: float32 [8, 1024], P('pipe'), may hold values from 0.1 to 1
- cotangent: bfloat16 [1024, 1024], P('dp'), may hold values from -0.119628906 to 0.119628906
- lengths: int32 [4, 2], P('dp'), may hold values from 1 to 128, 160 in all within a row
Outputs:
- weight_grad: bfloat16 [8, 2048, 1024], P('pipe', 'dp')
- gain_grad: float32 [8, 1024], P('pipe')
- scale_grad: float32 [8, 1024], P('pipe')
All inputs are finite; a program needn't handle non-finite values.
Results may differ from a plain program's by a relative error of at most 0.04.
Values may be sent and summed in bfloat16 or wider, within the bound.
No kernel may reach another device: no remote copies, remote signals or barrier semaphores. Data moves between devices by JAX's collectives and lax.ppermute only.
A program may use at most 64 MiB of HBM per device.

v0:
```python
import jax
import jax.numpy as jnp
from jax import lax
from jax.sharding import PartitionSpec as P

epsilon = 1e-06


def passed_along(block, axis, distance):
    devices = range(lax.axis_size(axis))
    route = [(i - distance, i) for i in devices if i - distance in devices]
    return lax.ppermute(block, axis, route)


def gelu_tanh(values):
    return jax.nn.gelu(values, approximate=True)


def layer_back(x_rows, incoming, up_weight, down_weight, gain_vec, scale_vec):
    x_float = x_rows.astype(jnp.float32)
    inverse = lax.rsqrt(jnp.mean(x_float * x_float, axis=-1, keepdims=True) + epsilon)
    unit = x_float * inverse
    normed = (unit * gain_vec).astype(jnp.bfloat16)
    hidden = jnp.dot(normed, up_weight, preferred_element_type=jnp.float32)
    active, gelu_back = jax.vjp(gelu_tanh, hidden)
    act = active.astype(jnp.bfloat16)
    branch = jnp.dot(act, down_weight, preferred_element_type=jnp.float32)
    upper = incoming.astype(jnp.float32)
    scale_part = jnp.sum(upper * branch, axis=0)
    branch_grad = (upper * scale_vec).astype(jnp.bfloat16)
    act_grad = jnp.dot(branch_grad, down_weight.T, preferred_element_type=jnp.float32)
    hidden_grad = gelu_back(act_grad)[0].astype(jnp.bfloat16)
    normed_grad = jnp.dot(hidden_grad, up_weight.T, preferred_element_type=jnp.float32)
    gain_part = jnp.sum(normed_grad * unit, axis=0)
    unit_grad = normed_grad * gain_vec
    back_rows = (
        upper + inverse * (unit_grad - unit * jnp.mean(unit_grad * unit, axis=-1, keepdims=True))
    ).astype(jnp.bfloat16)
    return (act, branch_grad, back_rows, gain_part, scale_part)


def shards(x_saved, up_weights, down_weights, norm_gain, layer_scale, cotangent, lengths):
    section_count = lax.axis_size("pipe")
    section_index = lax.axis_index("pipe")
    up_full, down_full = (
        lax.all_gather(up_weights, "dp", axis=1, tiled=True),
        lax.all_gather(down_weights, "dp", axis=1, tiled=True),
    )
    up_weight = up_full[0]
    down_weight = down_full[0]
    x_rows = x_saved[0]
    gain_vec = norm_gain[0]
    scale_vec = layer_scale[0]
    row_count = x_rows.shape[0]
    width = x_rows.shape[1]
    hidden_width = up_weight.shape[1]
    batches = lengths.shape[1]
    slot_rows = row_count // batches
    row_ids = jnp.arange(row_count, dtype=jnp.int32)
    position = row_ids % slot_rows
    owner = row_ids // slot_rows
    match = owner[:, None] == jnp.arange(batches, dtype=jnp.int32)[None, :]
    valid_len = jnp.sum(jnp.where(match, lengths[0][None, :], 0), axis=1)
    start_grad = jnp.where((position < valid_len)[:, None], cotangent, jnp.zeros_like(cotangent))
    pieces = 2 * batches
    piece_rows = row_count // pieces

    def step(step_index, carry):
        received, act_store, grad_store, acc_gain, acc_scale = carry
        piece_index = step_index - (section_count - 1 - section_index)
        working = jnp.logical_and(piece_index >= 0, piece_index < pieces)
        clamped = jnp.clip(piece_index, 0, pieces - 1)
        row_start = clamped * piece_rows
        x_piece = lax.dynamic_slice_in_dim(x_rows, row_start, piece_rows, 0)
        start_piece = lax.dynamic_slice_in_dim(start_grad, row_start, piece_rows, 0)
        incoming = jnp.where(section_index == section_count - 1, start_piece, received)

        def compute(unused):
            act, branch_grad, back_rows, gain_part, scale_part = layer_back(
                x_piece, incoming, up_weight, down_weight, gain_vec, scale_vec
            )
            new_act = lax.dynamic_update_slice_in_dim(act_store, act, row_start, 0)
            new_grad = lax.dynamic_update_slice_in_dim(grad_store, branch_grad, row_start, 0)
            return (back_rows, new_act, new_grad, acc_gain + gain_part, acc_scale + scale_part)

        def waiting(unused):
            return (jnp.zeros_like(received), act_store, grad_store, acc_gain, acc_scale)

        back_rows, act_store, grad_store, acc_gain, acc_scale = lax.cond(
            working, compute, waiting, 0
        )
        received = passed_along(back_rows, "pipe", -1)
        return (received, act_store, grad_store, acc_gain, acc_scale)

    start_carry = (
        jnp.zeros((piece_rows, width), jnp.bfloat16),
        jnp.zeros((row_count, hidden_width), jnp.bfloat16),
        jnp.zeros((row_count, width), jnp.bfloat16),
        jnp.zeros((width,), jnp.float32),
        jnp.zeros((width,), jnp.float32),
    )
    received, act_store, grad_store, acc_gain, acc_scale = lax.fori_loop(
        0, pieces + section_count - 1, step, start_carry
    )
    partial_grad = lax.dot_general(
        act_store, grad_store, (((0,), (0,)), ((), ())), preferred_element_type=jnp.float32
    ).astype(jnp.bfloat16)
    weight_part = lax.psum_scatter(partial_grad, "dp", scatter_dimension=0, tiled=True).astype(
        jnp.float32
    )
    gain_total, scale_total = lax.psum((acc_gain, acc_scale), "dp")
    return (weight_part.astype(jnp.bfloat16)[None], gain_total[None], scale_total[None])


def solution(mesh):
    return jax.shard_map(
        shards,
        mesh=mesh,
        in_specs=(
            P("pipe", "dp", None),
            P("pipe", "dp", None),
            P("pipe", "dp", None),
            P("pipe", None),
            P("pipe", None),
            P("dp", None),
            P("dp", None),
        ),
        out_specs=(P("pipe", "dp", None), P("pipe", None), P("pipe", None)),
        check_vma=False,
    )
```

profile of v0, /device:TPU:24, one launch (start us, length us, event | category | flops | bytes accessed | tf_op | source)
XLA Modules:
  0.0 460.7 jit_solution(4392076566480588698)
XLA Ops:
  7.2 0.7 all-gather.5.cloned.1.call-update
  7.9 0.0 all-gather.3.cloned.1.call-start
  8.0 0.7 all-gather.3.cloned.1.call-update
  8.7 0.0 reduce-scatter.2.cloned.1.call-start
  8.7 0.7 fusion.47
  9.5 1.1 broadcast_select_fusion
  10.6 78.0 %all-gather.5.cloned.1.call-done = bf16[1,1024,2048]{2,1,0:T(8,128)(2,1)} async-done(((bf16[1,256,2048]{2,1,0:T(8,128)(2,1)}), bf16[1,1024,2048]{2,1,0:T(8,128)(2,1)}) %all-gather.5.cloned.1.call-update) | async-done | bytes 4194320 | tf_op jit(solution)/shard_map/all_gather | solution.py:46
  88.6 80.9 %all-gather.3.cloned.1.call-done = bf16[1,2048,1024]{2,1,0:T(8,128)(2,1)} async-done(((bf16[1,512,1024]{2,1,0:T(8,128)(2,1)}), bf16[1,2048,1024]{2,1,0:T(8,128)(2,1)}) %all-gather.3.cloned.1.call-update) | async-done | bytes 4194320 | tf_op jit(solution)/shard_map/all_gather | solution.py:47
  169.6 0.9 broadcast.135
  170.4 0.1 broadcast_in_dim.39
  170.6 203.7 %while.23 = (s32[]{:T(128)}, bf16[64,1024]{1,0:T(8,128)(2,1)S(1)}, bf16[256,2048]{1,0:T(8,128)(2,1)S(1)}, bf16[256,1024]{1,0:T(8,128)(2,1)}, f32[1024]{0:T(1024)...) while((s32[]{:T(128)}, bf16[64,1024]{1,0:T(8,128)(2,1)S(1)}, ...), condition=%wide.region_8.9_spmd, body=%wide.region_1.8_spmd.sunk | while | flops 1080885248 | bytes 21291760 | solution.py:102
  170.6 1.3 collective-permute-start
  171.9 1.9 collective-permute-done
  173.9 1.3 collective-permute-start
  175.2 4.6 collective-permute-done
  179.8 1.3 collective-permute-start
  181.1 5.0 %collective-permute-done = bf16[64,1024]{1,0:T(8,128)(2,1)S(1)} collective-permute-done((bf16[64,1024]{1,0:T(8,128)(2,1)S(1)}, bf16[64,1024]{1,0:T(8,128)(2,1)S(1)}, u32[]{:S(2)}, u32[]{:S(2)}) %collective-permute-start) | collective-permute-done | bytes 131104 | tf_op jit(solution)/shard_map/while/body/eval_jaxpr/ppermute | solution.py:12
  186.1 1.3 collective-permute-start
  187.4 5.0 %collective-permute-done = bf16[64,1024]{1,0:T(8,128)(2,1)S(1)} collective-permute-done((bf16[64,1024]{1,0:T(8,128)(2,1)S(1)}, bf16[64,1024]{1,0:T(8,128)(2,1)S(1)}, u32[]{:S(2)}, u32[]{:S(2)}) %collective-permute-start) | collective-permute-done | bytes 131104 | tf_op jit(solution)/shard_map/while/body/eval_jaxpr/ppermute | solution.py:12
  192.5 1.3 collective-permute-start
  193.8 5.0 %collective-permute-done = bf16[64,1024]{1,0:T(8,128)(2,1)S(1)} collective-permute-done((bf16[64,1024]{1,0:T(8,128)(2,1)S(1)}, bf16[64,1024]{1,0:T(8,128)(2,1)S(1)}, u32[]{:S(2)}, u32[]{:S(2)}) %collective-permute-start) | collective-permute-done | bytes 131104 | tf_op jit(solution)/shard_map/while/body/eval_jaxpr/ppermute | solution.py:12
  198.8 1.3 collective-permute-start
  200.1 5.0 %collective-permute-done = bf16[64,1024]{1,0:T(8,128)(2,1)S(1)} collective-permute-done((bf16[64,1024]{1,0:T(8,128)(2,1)S(1)}, bf16[64,1024]{1,0:T(8,128)(2,1)S(1)}, u32[]{:S(2)}, u32[]{:S(2)}) %collective-permute-start) | collective-permute-done | bytes 131104 | tf_op jit(solution)/shard_map/while/body/eval_jaxpr/ppermute | solution.py:12
  205.1 1.3 collective-permute-start
  206.4 88.6 %collective-permute-done = bf16[64,1024]{1,0:T(8,128)(2,1)S(1)} collective-permute-done((bf16[64,1024]{1,0:T(8,128)(2,1)S(1)}, bf16[64,1024]{1,0:T(8,128)(2,1)S(1)}, u32[]{:S(2)}, u32[]{:S(2)}) %collective-permute-start) | collective-permute-done | bytes 131104 | tf_op jit(solution)/shard_map/while/body/eval_jaxpr/ppermute | solution.py:12
  295.0 13.6 %conditional.2 = (bf16[64,1024]{1,0:T(8,128)(2,1)S(1)}, bf16[256,2048]{1,0:T(8,128)(2,1)S(1)}, bf16[256,1024]{1,0:T(8,128)(2,1)}, f32[1024]{0:T(1024)S(1)}, f32[1024]{0:T(1024)S(1)}) conditional(s32[]{:T(128)} %convert_element_type.134, (bf16[256,2048]{1,0:T(8,128)(2,1)S(1)}, bf16[256,1024]{1,0:T(8,128)(2,1)}, f32[1024]{0:T(1024)S(1)}, ...), branch_computations={%region_2.2_spmd, %region_3.7_spmd} | conditional | flops 1080885248 | bytes 20767102 | solution.py:89
  295.0 0.1 fusion.17
  295.1 0.7 fusion.32
  295.8 3.2 constant_dynamic-update-slice_fusion
  299.0 6.3 %fusion.16 = (f32[1024]{0:T(1024)S(1)}, f32[64]{0:T(128)S(1)}, f32[64,1024]{1,0:T(8,128)S(1)}) fusion(f32[64]{0:T(128)S(1)} %add_rsqrt_fusion, bf16[256,1024]{1,0:T(8,128)(2,1)S(1)} %get-tuple-element.487, s32[]{:T(128)S(6)} %select_n.70, f32[1024]{0:T(1024)S(1)} %bitcast.19, bf16[1024,2048]{1,0:T(8,128)(2,1)} %get-tuple-element.491, ...), kind=kOutput, calls=%fused_computation.24 | convolution fusion | flops 540146624 | bytes 9449988 | tf_op jit(solution)/shard_map/while/body/eval_jaxpr/cond/branch_1_fun/dot_general | solution.py:33
  305.3 3.0 fusion
  308.4 0.2 fusion.19
  308.6 1.3 collective-permute-start
  309.9 5.9 %collective-permute-done = bf16[64,1024]{1,0:T(8,128)(2,1)S(1)} collective-permute-done((bf16[64,1024]{1,0:T(8,128)(2,1)S(1)}, bf16[64,1024]{1,0:T(8,128)(2,1)S(1)}, u32[]{:S(2)}, u32[]{:S(2)}) %collective-permute-start) | collective-permute-done | bytes 131104 | tf_op jit(solution)/shard_map/while/body/eval_jaxpr/ppermute | solution.py:12
  315.8 13.6 %conditional.2 = (bf16[64,1024]{1,0:T(8,128)(2,1)S(1)}, bf16[256,2048]{1,0:T(8,128)(2,1)S(1)}, bf16[256,1024]{1,0:T(8,128)(2,1)}, f32[1024]{0:T(1024)S(1)}, f32[1024]{0:T(1024)S(1)}) conditional(s32[]{:T(128)} %convert_element_type.134, (bf16[256,2048]{1,0:T(8,128)(2,1)S(1)}, bf16[256,1024]{1,0:T(8,128)(2,1)}, f32[1024]{0:T(1024)S(1)}, ...), branch_computations={%region_2.2_spmd, %region_3.7_spmd} | conditional | flops 1080885248 | bytes 20767102 | solution.py:89
  315.8 0.1 fusion.17
  315.9 0.7 fusion.32
  316.6 3.2 constant_dynamic-update-slice_fusion
  319.8 6.3 %fusion.16 = (f32[1024]{0:T(1024)S(1)}, f32[64]{0:T(128)S(1)}, f32[64,1024]{1,0:T(8,128)S(1)}) fusion(f32[64]{0:T(128)S(1)} %add_rsqrt_fusion, bf16[256,1024]{1,0:T(8,128)(2,1)S(1)} %get-tuple-element.487, s32[]{:T(128)S(6)} %select_n.70, f32[1024]{0:T(1024)S(1)} %bitcast.19, bf16[1024,2048]{1,0:T(8,128)(2,1)} %get-tuple-element.491, ...), kind=kOutput, calls=%fused_computation.24 | convolution fusion | flops 540146624 | bytes 9449988 | tf_op jit(solution)/shard_map/while/body/eval_jaxpr/cond/branch_1_fun/dot_general | solution.py:33
  326.1 3.0 fusion
  329.2 0.2 fusion.19
  329.4 1.3 collective-permute-start
  330.7 5.9 %collective-permute-done = bf16[64,1024]{1,0:T(8,128)(2,1)S(1)} collective-permute-done((bf16[64,1024]{1,0:T(8,128)(2,1)S(1)}, bf16[64,1024]{1,0:T(8,128)(2,1)S(1)}, u32[]{:S(2)}, u32[]{:S(2)}) %collective-permute-start) | collective-permute-done | bytes 131104 | tf_op jit(solution)/shard_map/while/body/eval_jaxpr/ppermute | solution.py:12
  336.6 13.6 %conditional.2 = (bf16[64,1024]{1,0:T(8,128)(2,1)S(1)}, bf16[256,2048]{1,0:T(8,128)(2,1)S(1)}, bf16[256,1024]{1,0:T(8,128)(2,1)}, f32[1024]{0:T(1024)S(1)}, f32[1024]{0:T(1024)S(1)}) conditional(s32[]{:T(128)} %convert_element_type.134, (bf16[256,2048]{1,0:T(8,128)(2,1)S(1)}, bf16[256,1024]{1,0:T(8,128)(2,1)}, f32[1024]{0:T(1024)S(1)}, ...), branch_computations={%region_2.2_spmd, %region_3.7_spmd} | conditional | flops 1080885248 | bytes 20767102 | solution.py:89
  336.6 0.1 fusion.17
  336.7 0.7 fusion.32
  337.4 3.2 constant_dynamic-update-slice_fusion
  340.6 6.3 %fusion.16 = (f32[1024]{0:T(1024)S(1)}, f32[64]{0:T(128)S(1)}, f32[64,1024]{1,0:T(8,128)S(1)}) fusion(f32[64]{0:T(128)S(1)} %add_rsqrt_fusion, bf16[256,1024]{1,0:T(8,128)(2,1)S(1)} %get-tuple-element.487, s32[]{:T(128)S(6)} %select_n.70, f32[1024]{0:T(1024)S(1)} %bitcast.19, bf16[1024,2048]{1,0:T(8,128)(2,1)} %get-tuple-element.491, ...), kind=kOutput, calls=%fused_computation.24 | convolution fusion | flops 540146624 | bytes 9449988 | tf_op jit(solution)/shard_map/while/body/eval_jaxpr/cond/branch_1_fun/dot_general | solution.py:33
  346.9 3.0 fusion
  350.0 0.2 fusion.19
  350.2 1.3 collective-permute-start
  351.5 5.9 %collective-permute-done = bf16[64,1024]{1,0:T(8,128)(2,1)S(1)} collective-permute-done((bf16[64,1024]{1,0:T(8,128)(2,1)S(1)}, bf16[64,1024]{1,0:T(8,128)(2,1)S(1)}, u32[]{:S(2)}, u32[]{:S(2)}) %collective-permute-start) | collective-permute-done | bytes 131104 | tf_op jit(solution)/shard_map/while/body/eval_jaxpr/ppermute | solution.py:12
  357.4 13.6 %conditional.2 = (bf16[64,1024]{1,0:T(8,128)(2,1)S(1)}, bf16[256,2048]{1,0:T(8,128)(2,1)S(1)}, bf16[256,1024]{1,0:T(8,128)(2,1)}, f32[1024]{0:T(1024)S(1)}, f32[1024]{0:T(1024)S(1)}) conditional(s32[]{:T(128)} %convert_element_type.134, (bf16[256,2048]{1,0:T(8,128)(2,1)S(1)}, bf16[256,1024]{1,0:T(8,128)(2,1)}, f32[1024]{0:T(1024)S(1)}, ...), branch_computations={%region_2.2_spmd, %region_3.7_spmd} | conditional | flops 1080885248 | bytes 20767102 | solution.py:89
  357.4 0.1 fusion.17
  357.5 0.7 fusion.32
  358.2 3.2 constant_dynamic-update-slice_fusion
  361.4 6.3 %fusion.16 = (f32[1024]{0:T(1024)S(1)}, f32[64]{0:T(128)S(1)}, f32[64,1024]{1,0:T(8,128)S(1)}) fusion(f32[64]{0:T(128)S(1)} %add_rsqrt_fusion, bf16[256,1024]{1,0:T(8,128)(2,1)S(1)} %get-tuple-element.487, s32[]{:T(128)S(6)} %select_n.70, f32[1024]{0:T(1024)S(1)} %bitcast.19, bf16[1024,2048]{1,0:T(8,128)(2,1)} %get-tuple-element.491, ...), kind=kOutput, calls=%fused_computation.24 | convolution fusion | flops 540146624 | bytes 9449988 | tf_op jit(solution)/shard_map/while/body/eval_jaxpr/cond/branch_1_fun/dot_general | solution.py:33
  367.7 3.0 fusion
  370.8 0.2 fusion.19
  371.0 1.3 collective-permute-start
  372.3 1.9 collective-permute-done
  374.2 4.3 convolution_convert_fusion
  378.5 12.8 %all-reduce = (f32[1,1024]{1,0:T(1,128)}, f32[1,1024]{1,0:T(1,128)}) all-reduce(f32[1,1024]{1,0:T(1,128)S(1)} %bitcast.24, f32[1,1024]{1,0:T(1,128)S(1)} %bitcast.23), channel_id=1, replica_groups=mesh['pipe'=8,'dp'=4] {'dp'}, use_global_device_ids=true, to_apply=%region_10.11 | all-reduce | flops 2048 | bytes 16384 | tf_op jit(solution)/shard_map/psum | solution.py:111
  391.3 62.8 %reduce-scatter.2.cloned.1.call-done = bf16[512,1024]{1,0:T(8,128)(2,1)} async-done(((bf16[2048,1024]{1,0:T(8,128)(2,1)}), bf16[512,1024]{1,0:T(8,128)(2,1)}) %reduce-scatter.2.cloned.1.call-update) | async-done | bytes 1048592 | tf_op jit(solution)/shard_map/reduce_scatter | solution.py:108
  (43 shorter events, 0.5 us)
Async XLA Ops:
  7.2 163.4 %copy-start.2 = (f32[1,1024]{1,0:T(1,128)S(1)}, f32[1,1024]{1,0:T(1,128)}, u32[]{:S(2)}) copy-start(f32[1,1024]{1,0:T(1,128)} %param.15) | copy-start | bytes 12292
  7.2 163.4 %copy-start.1 = (f32[1,1024]{1,0:T(1,128)S(1)}, f32[1,1024]{1,0:T(1,128)}, u32[]{:S(2)}) copy-start(f32[1,1024]{1,0:T(1,128)} %param.14) | copy-start | bytes 12292
  7.2 163.4 %copy-start = (bf16[1,256,1024]{2,1,0:T(8,128)(2,1)S(1)}, bf16[1,256,1024]{2,1,0:T(8,128)(2,1)}, u32[]{:S(2)}) copy-start(bf16[1,256,1024]{2,1,0:T(8,128)(2,1)} %param.11) | copy-start | bytes 1572868
  7.2 81.4 %all-gather.5.cloned.1.call-start = ((), (), s32[]{:S(2)}) async-start(), calls=%async_computation.2 | async-start | bytes 5242880 | tf_op jit(solution)/shard_map/all_gather | solution.py:46
  7.9 161.6 %all-gather.3.cloned.1.call-start = ((), (), s32[]{:S(2)}) async-start(), calls=%async_computation.1 | async-start | bytes 5242880 | tf_op jit(solution)/shard_map/all_gather | solution.py:47
  8.7 445.4 %reduce-scatter.2.cloned.1.call-start = ((), (), s32[]{:S(2)}) async-start(), calls=%async_computation.3 | async-start | bytes 5242880 | tf_op jit(solution)/shard_map/reduce_scatter | solution.py:108
  170.6 3.2 collective-permute-start
  173.9 5.9 %collective-permute-start = (bf16[64,1024]{1,0:T(8,128)(2,1)S(1)}, bf16[64,1024]{1,0:T(8,128)(2,1)S(1)}, u32[]{:S(2)}, u32[]{:S(2)}) collective-permute-start(bf16[64,1024]{1,0:T(8,128)(2,1)S(1)} %get-tuple-element.654), channel_id=1, source_target_pairs={{4,0},{8,4},{12,8},{16,12},{20,16},{24,20},{28,24},{5,1},{9,5},{13... | collective-permute-start | bytes 393224 | tf_op jit(solution)/shard_map/while/body/eval_jaxpr/ppermute | solution.py:12
  179.8 6.3 %collective-permute-start = (bf16[64,1024]{1,0:T(8,128)(2,1)S(1)}, bf16[64,1024]{1,0:T(8,128)(2,1)S(1)}, u32[]{:S(2)}, u32[]{:S(2)}) collective-permute-start(bf16[64,1024]{1,0:T(8,128)(2,1)S(1)} %get-tuple-element.654), channel_id=1, source_target_pairs={{4,0},{8,4},{12,8},{16,12},{20,16},{24,20},{28,24},{5,1},{9,5},{13... | collective-permute-start | bytes 393224 | tf_op jit(solution)/shard_map/while/body/eval_jaxpr/ppermute | solution.py:12
  186.1 6.3 %collective-permute-start = (bf16[64,1024]{1,0:T(8,128)(2,1)S(1)}, bf16[64,1024]{1,0:T(8,128)(2,1)S(1)}, u32[]{:S(2)}, u32[]{:S(2)}) collective-permute-start(bf16[64,1024]{1,0:T(8,128)(2,1)S(1)} %get-tuple-element.654), channel_id=1, source_target_pairs={{4,0},{8,4},{12,8},{16,12},{20,16},{24,20},{28,24},{5,1},{9,5},{13... | collective-permute-start | bytes 393224 | tf_op jit(solution)/shard_map/while/body/eval_jaxpr/ppermute | solution.py:12
  192.5 6.3 %collective-permute-start = (bf16[64,1024]{1,0:T(8,128)(2,1)S(1)}, bf16[64,1024]{1,0:T(8,128)(2,1)S(1)}, u32[]{:S(2)}, u32[]{:S(2)}) collective-permute-start(bf16[64,1024]{1,0:T(8,128)(2,1)S(1)} %get-tuple-element.654), channel_id=1, source_target_pairs={{4,0},{8,4},{12,8},{16,12},{20,16},{24,20},{28,24},{5,1},{9,5},{13... | collective-permute-start | bytes 393224 | tf_op jit(solution)/shard_map/while/body/eval_jaxpr/ppermute | solution.py:12
  198.8 6.3 %collective-permute-start = (bf16[64,1024]{1,0:T(8,128)(2,1)S(1)}, bf16[64,1024]{1,0:T(8,128)(2,1)S(1)}, u32[]{:S(2)}, u32[]{:S(2)}) collective-permute-start(bf16[64,1024]{1,0:T(8,128)(2,1)S(1)} %get-tuple-element.654), channel_id=1, source_target_pairs={{4,0},{8,4},{12,8},{16,12},{20,16},{24,20},{28,24},{5,1},{9,5},{13... | collective-permute-start | bytes 393224 | tf_op jit(solution)/shard_map/while/body/eval_jaxpr/ppermute | solution.py:12
  205.1 89.9 %collective-permute-start = (bf16[64,1024]{1,0:T(8,128)(2,1)S(1)}, bf16[64,1024]{1,0:T(8,128)(2,1)S(1)}, u32[]{:S(2)}, u32[]{:S(2)}) collective-permute-start(bf16[64,1024]{1,0:T(8,128)(2,1)S(1)} %get-tuple-element.654), channel_id=1, source_target_pairs={{4,0},{8,4},{12,8},{16,12},{20,16},{24,20},{28,24},{5,1},{9,5},{13... | collective-permute-start | bytes 393224 | tf_op jit(solution)/shard_map/while/body/eval_jaxpr/ppermute | solution.py:12
  308.6 7.2 %collective-permute-start = (bf16[64,1024]{1,0:T(8,128)(2,1)S(1)}, bf16[64,1024]{1,0:T(8,128)(2,1)S(1)}, u32[]{:S(2)}, u32[]{:S(2)}) collective-permute-start(bf16[64,1024]{1,0:T(8,128)(2,1)S(1)} %get-tuple-element.654), channel_id=1, source_target_pairs={{4,0},{8,4},{12,8},{16,12},{20,16},{24,20},{28,24},{5,1},{9,5},{13... | collective-permute-start | bytes 393224 | tf_op jit(solution)/shard_map/while/body/eval_jaxpr/ppermute | solution.py:12
  329.4 7.2 %collective-permute-start = (bf16[64,1024]{1,0:T(8,128)(2,1)S(1)}, bf16[64,1024]{1,0:T(8,128)(2,1)S(1)}, u32[]{:S(2)}, u32[]{:S(2)}) collective-permute-start(bf16[64,1024]{1,0:T(8,128)(2,1)S(1)} %get-tuple-element.654), channel_id=1, source_target_pairs={{4,0},{8,4},{12,8},{16,12},{20,16},{24,20},{28,24},{5,1},{9,5},{13... | collective-permute-start | bytes 393224 | tf_op jit(solution)/shard_map/while/body/eval_jaxpr/ppermute | solution.py:12
  350.2 7.2 %collective-permute-start = (bf16[64,1024]{1,0:T(8,128)(2,1)S(1)}, bf16[64,1024]{1,0:T(8,128)(2,1)S(1)}, u32[]{:S(2)}, u32[]{:S(2)}) collective-permute-start(bf16[64,1024]{1,0:T(8,128)(2,1)S(1)} %get-tuple-element.654), channel_id=1, source_target_pairs={{4,0},{8,4},{12,8},{16,12},{20,16},{24,20},{28,24},{5,1},{9,5},{13... | collective-permute-start | bytes 393224 | tf_op jit(solution)/shard_map/while/body/eval_jaxpr/ppermute | solution.py:12
  371.0 3.2 collective-permute-start
Sparse Core Ops, SparseCore 0:
  9.6 78.9 all-gather.4
  90.2 79.2 all-gather.2
  378.6 75.4 reduce-scatter.1
where the time goes:
time: 464 us; the launch traced here: 461 us
  waiting for transfers between devices  358 us (77%)
  matrix products  54.4 us (12%)
  starting transfers between devices  14.3 us (3%)
  between operations  13.8 us (3%)
  blocking collectives  12.8 us (3%)
  other arithmetic  6 us (1%)
    ppermute x11, waiting for transfers between devices, passed_along(): return lax.ppermute(block, axis, route)  135 us
    all_gather x1, waiting for transfers between devices, shards(): lax.all_gather(down_weights, 'dp', axis=1, tiled=True)  80.9 us
    all_gather x1, waiting for transfers between devices, shards(): lax.all_gather(up_weights, 'dp', axis=1, tiled=True)  78 us
    reduce_scatter x1, waiting for transfers between devices, shards(): lax.psum_scatter(partial_grad, 'dp', scatter_dimension=0, tiled=True)  62.8 us
    dot_general x4, matrix products, layer_back(): jnp.dot(hidden_grad, up_weight.T, preferred_element_type=jnp.float32)  25.3 us
    ppermute x11, starting transfers between devices, passed_along(): return lax.ppermute(block, axis, route)  14.2 us
    psum x1, blocking collectives, shards(): gain_total, scale_total = lax.psum((acc_gain, acc_scale), 'dp')  12.8 us
    dot_general x4, matrix products, layer_back(): hidden = jnp.dot(normed, up_weight, preferred_element_type=jnp.float32)  12.7 us
  transfers between devices with their start and end apart: 14, of which 14 were waited for; matrix products, arithmetic and copies ran while one was open for 0% of the time, Pallas kernels for 0%

commit v1 on v0

v1 whole, which is shorter than its diff:
```python
import functools
import math

import jax
import jax.numpy as jnp
from jax import lax
from jax.experimental import pallas as pl
from jax.experimental.pallas import tpu as pltpu
from jax.sharding import PartitionSpec as P

epsilon = 1e-06
slope = math.sqrt(2.0 / math.pi)
cubic = 0.044715
NT = (((1,), (1,)), ((), ()))
axes = ("pipe", "dp")
in_vmem = pl.BlockSpec(memory_space=pltpu.VMEM)
in_smem = pl.BlockSpec(memory_space=pltpu.SMEM)


def held(array):
    return pltpu.with_memory_space_constraint(array, pltpu.VMEM)


def home_of(section, lines):
    middle = lines // 2
    return middle if ((section + 1) // 2) % 2 == 0 else max(middle - 1, 0)


def hidden_kernel(parts, piece_rows, x_ref, gain_ref, *refs):
    up_refs, (act_ref, slope_ref) = refs[:parts], refs[parts:]
    depth, wide = up_refs[0].shape
    chunk = math.gcd(wide, 512)

    @pl.loop(0, x_ref.shape[0] // piece_rows)
    def piece(index):
        rows = pl.ds(pl.multiple_of(index * piece_rows, piece_rows), piece_rows)
        x = x_ref[rows, :].astype(jnp.float32)
        inverse = lax.rsqrt(jnp.mean(x * x, axis=-1, keepdims=True) + epsilon)
        normed = (x * inverse * gain_ref[...]).astype(jnp.bfloat16)
        for start in range(0, wide, chunk):
            hidden = jnp.zeros((piece_rows, chunk), jnp.float32)
            for part in range(parts):
                hidden += jnp.dot(
                    normed[:, part * depth : (part + 1) * depth],
                    up_refs[part][:, start : start + chunk],
                    preferred_element_type=jnp.float32,
                )
            square = hidden * hidden
            bent = jnp.tanh(slope * hidden * (1.0 + cubic * square))
            half = 0.5 + 0.5 * bent
            act_ref[rows, start : start + chunk] = (hidden * half).astype(jnp.bfloat16)
            rise = half + (0.5 * slope) * hidden * (1.0 - bent * bent) * (1.0 + (3.0 * cubic) * square)
            slope_ref[rows, start : start + chunk] = rise.astype(jnp.bfloat16)


def chain_kernel(parts, piece_rows, plan_ref, recv_ref, x_ref, slope_ref, gain_ref, scale_ref, *refs):
    up_refs, down_refs = refs[:parts], refs[parts : 2 * parts]
    store_in, total_in, back_ref, store_ref, total_ref = refs[2 * parts :]
    width = x_ref.shape[1]

    @pl.when(plan_ref[1] == 1)
    def active():
        rows = pl.ds(pl.multiple_of(plan_ref[0] * piece_rows, piece_rows), piece_rows)

        @pl.when(plan_ref[2] == 0)
        def received():
            store_ref[rows, :] = recv_ref[...]

        upper = store_ref[rows, :].astype(jnp.float32)
        branch_grad = (upper * scale_ref[...]).astype(jnp.bfloat16)
        pieces = []
        for part in range(parts):
            block = down_refs[part].shape[0]
            grown = lax.dot_general(branch_grad, down_refs[part][...], NT, preferred_element_type=jnp.float32)
            rise = slope_ref[rows, part * block : (part + 1) * block].astype(jnp.float32)
            pieces.append((grown * rise).astype(jnp.bfloat16))
        hidden_grad = jnp.concatenate(pieces, axis=1)
        x = x_ref[rows, :].astype(jnp.float32)
        inverse = lax.rsqrt(jnp.mean(x * x, axis=-1, keepdims=True) + epsilon)
        unit = x * inverse
        normed_grad = jnp.concatenate(
            [
                lax.dot_general(hidden_grad, up_refs[part][...], NT, preferred_element_type=jnp.float32)
                for part in range(parts)
            ],
            axis=1,
        )
        total_ref[...] += jnp.sum(normed_grad * unit, axis=0, keepdims=True)
        unit_grad = normed_grad * gain_ref[...]
        mean = jnp.sum(unit_grad * unit, axis=-1, keepdims=True) * (1.0 / width)
        back_ref[...] = (upper + inverse * (unit_grad - unit * mean)).astype(jnp.bfloat16)


def shards(x_saved, up_weights, down_weights, norm_gain, layer_scale, cotangent, lengths):
    sections, lines = lax.axis_size("pipe"), lax.axis_size("dp")
    section, line = lax.axis_index("pipe"), lax.axis_index("dp")
    row_count, width = cotangent.shape
    wide = up_weights.shape[2]
    batches = lengths.shape[1]
    slot_rows = row_count // batches
    piece_rows = row_count * 5 // 8
    gain, scale = norm_gain, layer_scale

    def device(p, z):
        return p * lines + z

    def home(p):
        return home_of(p, lines)

    def to_home(array, source, layers):
        return lax.ppermute(array, axes, [(device(p, source), device(p, home(p))) for p in layers])

    def from_home(array, target):
        return lax.ppermute(array, axes, [(device(p, home(p)), device(p, target)) for p in range(sections)])

    ends = jnp.cumsum(lengths[0])
    pack_ids = jnp.arange(piece_rows, dtype=jnp.int32)
    owner = jnp.sum(pack_ids[:, None] >= ends[None, :], axis=1)
    starts = ends - lengths[0]
    chosen = owner[:, None] == jnp.arange(batches, dtype=jnp.int32)[None, :]
    offset = jnp.sum(jnp.where(chosen, starts[None, :], 0), axis=1)
    source_row = owner * slot_rows + pack_ids - offset
    picker = (source_row[:, None] == jnp.arange(row_count, dtype=jnp.int32)[None, :]).astype(jnp.bfloat16)

    def packed(rows):
        return jnp.dot(picker, rows, preferred_element_type=jnp.float32).astype(jnp.bfloat16)

    every = range(sections)
    x_pack, start_pack = packed(x_saved[0]), packed(cotangent)
    x_all = jnp.concatenate([to_home(x_pack, z, every) for z in range(lines)], axis=0)
    ups = [to_home(up_weights[0], z, every) for z in range(lines)]
    store = jnp.concatenate([to_home(start_pack, z, [sections - 1]) for z in range(lines)], axis=0)
    downs = [to_home(down_weights[0], z, every) for z in range(lines)]

    x_held, up_held, down_held = held(x_all), [held(u) for u in ups], [held(d) for d in downs]
    total_rows = lines * piece_rows
    act, rise = pl.pallas_call(
        functools.partial(hidden_kernel, lines, piece_rows),
        out_shape=[jax.ShapeDtypeStruct((total_rows, wide), jnp.bfloat16)] * 2,
        in_specs=[in_vmem] * (2 + lines),
        out_specs=[in_vmem] * 2,
        compiler_params=pltpu.CompilerParams(vmem_limit_bytes=16 << 20),
        name="hidden",
    )(x_held, gain, *up_held)
    rise = held(rise)

    total = jnp.zeros((1, width), jnp.float32)
    received = jnp.zeros((piece_rows, width), jnp.bfloat16)
    first = (section == sections - 1).astype(jnp.int32)
    at_home = jnp.zeros((), jnp.bool_)
    for p in every:
        at_home = jnp.logical_or(at_home, jnp.logical_and(section == p, line == home(p)))
    steps = sections + lines - 1
    chain = pl.pallas_call(
        functools.partial(chain_kernel, lines, piece_rows),
        out_shape=[
            jax.ShapeDtypeStruct((piece_rows, width), jnp.bfloat16),
            jax.ShapeDtypeStruct((total_rows, width), jnp.bfloat16),
            jax.ShapeDtypeStruct((1, width), jnp.float32),
        ],
        in_specs=[in_smem] + [in_vmem] * (7 + 2 * lines),
        out_specs=[in_vmem] * 3,
        input_output_aliases={6 + 2 * lines: 1, 7 + 2 * lines: 2},
        compiler_params=pltpu.CompilerParams(vmem_limit_bytes=16 << 20),
        name="chain",
    )
    for step in range(steps):
        piece = step - (sections - 1 - section)
        working = jnp.logical_and(at_home, jnp.logical_and(piece >= 0, piece < lines))
        plan = jnp.stack([jnp.clip(piece, 0, lines - 1), working.astype(jnp.int32), first])
        back, store, total = chain(
            plan, held(received), x_held, rise, gain, scale, *up_held, *down_held, held(store), held(total)
        )
        moving = [p for p in range(1, sections) if 0 <= step - (sections - 1 - p) < lines]
        if moving:
            received = lax.ppermute(
                back, axes, [(device(p, home(p)), device(p - 1, home(p - 1))) for p in moving]
            )

    block = wide // lines
    scale_part = jnp.zeros((1, width), jnp.float32)
    weight_part = None
    for z in range(lines):
        grown = lax.dot_general(
            act[:, z * block : (z + 1) * block], store, (((0,), (0,)), ((), ())), preferred_element_type=jnp.float32
        )
        scale_part += jnp.sum(grown * downs[z].astype(jnp.float32), axis=0, keepdims=True)
        moved = from_home((grown * scale).astype(jnp.bfloat16), z)
        weight_part = moved if weight_part is None else weight_part + moved
    sums = jnp.concatenate([total, scale_part], axis=0)
    spread = sum(from_home(sums, z) for z in range(lines))
    return (weight_part[None], spread[0:1], spread[1:2])


def solution(mesh):
    return jax.shard_map(
        shards,
        mesh=mesh,
        in_specs=(
            P("pipe", "dp", None),
            P("pipe", "dp", None),
            P("pipe", "dp", None),
            P("pipe", None),
            P("pipe", None),
            P("dp", None),
            P("dp", None),
        ),
        out_specs=(P("pipe", "dp", None), P("pipe", None), P("pipe", None)),
        check_vma=False,
    )
```

time: 464 us -> 382 us (0.82)
  waiting for transfers between devices: 358 us -> 169 us
  local copies, waits for them, and re-layouts: 1.07 us -> 101 us
  matrix products: 54.4 us -> 10.8 us
  Pallas kernels: 0 us -> 39.5 us
  starting transfers between devices: 14.3 us -> 52 us
  blocking collectives: 12.8 us -> 0 us
  between operations: 13.8 us -> 1.44 us
    all_gather x2 -> x0, waiting for transfers between devices: 159 us -> none  [the longest x1 80.9 us: shards(): lax.all_gather(down_weights, 'dp', axis=1, tiled=True)]
    unnamed x6 -> x193, local copies, waits for them, and re-layouts: 0.01 us -> 101 us
    reduce_scatter x1 -> x0, waiting for transfers between devices: 62.8 us -> none  [shards(): lax.psum_scatter(partial_grad, 'dp', scatter_dimension=0, tiled=True)]
    dot_general x13 -> x6, matrix products: 54.4 us -> 10.8 us  [the longest x4 9.19 us: shards(): lax.dot_general(act[:, z * block:(z + 1) * block], store, (((0,), (0,)),...]
    pallas_call x0 -> x12, Pallas kernels: none -> 39.5 us  [the longest x11 33.1 us: shards(): chain(plan, held(received), x_held, rise, gain, scale, *up_held, *down_he...]
    ppermute x11 -> x34, starting transfers between devices: 14.2 us -> 52 us  [the longest x16 38.6 us: to_home(): lax.ppermute(array, axes, [(device(p, source), device(p, home(p))) for p...]
    ppermute x11 -> x34, waiting for transfers between devices: 135 us -> 169 us  [the longest x8 155 us: from_home(): lax.ppermute(array, axes, [(device(p, home(p)), device(p, target)) for p...]
    psum x1 -> x0, blocking collectives: 12.8 us -> none  [shards(): gain_total, scale_total = lax.psum((acc_gain, acc_scale), 'dp')]
  transfers between devices with their start and end apart: 14 -> 34, of which waited for: 14 -> 4; matrix products, arithmetic and copies ran while one was open for 0% -> 3% of each run, Pallas kernels for 0% -> 2%
where the time goes in v1:
time: 382 us; the launch traced here: 378 us
  waiting for transfers between devices  169 us (44%)
  local copies, waits for them, and re-layouts  101 us (26%)
  starting transfers between devices  52 us (14%)
  Pallas kernels  39.5 us (10%)
  matrix products  10.8 us (3%)
  other arithmetic  3.93 us (1%)
    ppermute x8, waiting for transfers between devices, from_home(): lax.ppermute(array, axes, [(device(p, home(p)), device(p, target)) for p...  155 us
    unnamed x193, local copies, waits for them, and re-layouts  101 us
    ppermute x16, starting transfers between devices, to_home(): lax.ppermute(array, axes, [(device(p, source), device(p, home(p))) for p...  38.6 us
    pallas_call x11, Pallas kernels, shards(): chain(plan, held(received), x_held, rise, gain, scale, *up_held, *down_he...  33.1 us
    ppermute x16, waiting for transfers between devices, to_home(): lax.ppermute(array, axes, [(device(p, source), device(p, home(p))) for p...  13.7 us
    dot_general x4, matrix products, shards(): lax.dot_general(act[:, z * block:(z + 1) * block], store, (((0,), (0,)),...  9.19 us
  transfers between devices with their start and end apart: 34, of which 4 were waited for; matrix products, arithmetic and copies ran while one was open for 3% of the time, Pallas kernels for 2%

profile of v1, /device:TPU:24, one launch (start us, length us, event | category | flops | bytes accessed | tf_op | source)
XLA Modules:
  0.0 378.4 jit_solution(8750955728140290894)
XLA Ops:
  7.0 12.2 %collective-permute-start.3 = (bf16[160,1024]{1,0:T(8,128)(2,1)S(1)}, bf16[160,1024]{1,0:T(8,128)(2,1)S(1)}, u32[]{:S(2)}, u32[]{:S(2)}) collective-permute-start(bf16[160,1024]{1,0:T(8,128)(2,1)S(1)} %convolution_convert_fusion.1), channel_id=1, source_target_pairs={{3,2},{7,5},{11,9},{15,14},{19,18},{23,21},{27,25},{31,30}} | collective-permute-start | bytes 983048 | tf_op jit(solution)/shard_map/ppermute | solution.py:111
  19.2 1.3 convolution_convert_fusion
  21.2 2.5 collective-permute-done.3
  25.8 4.5 %collective-permute-start.7 = (bf16[256,2048]{1,0:T(8,128)(2,1)}, bf16[256,2048]{1,0:T(8,128)(2,1)S(1)}, u32[]{:S(2)}, u32[]{:S(2)}) collective-permute-start(bf16[256,2048]{1,0:T(8,128)(2,1)} %bitcast.5), channel_id=1, source_target_pairs={{3,2},{7,5},{11,9},{15,14},{19,18},{23,21},{27,25},{31,30}} | collective-permute-start | bytes 3145736 | tf_op jit(solution)/shard_map/ppermute | solution.py:111
  30.3 1.6 collective-permute-start.10
  32.9 10.0 %collective-permute-start.11 = (bf16[512,1024]{1,0:T(8,128)(2,1)}, bf16[512,1024]{1,0:T(8,128)(2,1)}, u32[]{:S(2)}, u32[]{:S(2)}) collective-permute-start(bf16[512,1024]{1,0:T(8,128)(2,1)} %bitcast.29), channel_id=1, source_target_pairs={{3,2},{7,5},{11,9},{15,14},{19,18},{23,21},{27,25},{31,30}} | collective-permute-start | bytes 3145736 | tf_op jit(solution)/shard_map/ppermute | solution.py:111
  43.9 1.7 collective-permute-start.8
  46.6 1.7 collective-permute-start.9
  52.1 1.2 copy-done.76
  53.3 6.4 %hidden.1 = (bf16[640,2048]{1,0:T(8,128)(2,1)S(1)}, bf16[640,2048]{1,0:T(8,128)(2,1)S(1)}) custom-call(bf16[640,1024]{1,0:T(8,128)(2,1)S(1)} %constant_dynamic-update-slice_fusion.x_ref, f32[1,1024]{1,0:T(1,128)S(1)} %copy-done.87, bf16[256,2048]{1,0:T(8,128)(2,1)S(1)} %copy-done.40, bf16[256,2048]{1,0:T(8,128)(2,1)S(1)} %copy-done.52, ...), custom_call_target="tpu_custom_call" | custom-call | tf_op jit(solution)/shard_map/hidden/pallas_call | solution.py:137
  59.7 1.5 copy-done.89
  61.2 11.0 %collective-permute-done.11.refs_7_ = bf16[512,1024]{1,0:T(8,128)(2,1)} collective-permute-done((bf16[512,1024]{1,0:T(8,128)(2,1)}, bf16[512,1024]{1,0:T(8,128)(2,1)}, u32[]{:S(2)}, u32[]{:S(2)}) %collective-permute-start.11) | collective-permute-done | bytes 1048608 | tf_op jit(solution)/shard_map/ppermute | solution.py:111
  72.3 2.9 chain.11
  77.1 1.7 copy-done.2
  78.8 1.3 copy-done.9
  80.2 1.3 copy-done.20
  81.5 1.2 copy-done.41
  82.7 1.2 copy-done.53
  83.9 1.2 copy-done.65
  86.4 3.1 chain.12
  91.4 1.3 copy-done.10
  92.7 1.3 copy-done.22
  94.0 1.2 copy-done.42
  95.2 1.2 copy-done.54
  96.4 1.2 copy-done.66
  97.7 1.2 copy-done.78
  98.9 2.9 chain.13
  103.7 1.7 copy-done.4
  105.5 1.3 copy-done.11
  106.8 1.3 copy-done.24
  108.1 1.2 copy-done.43
  109.3 1.2 copy-done.55
  113.0 3.2 chain.14
  118.2 1.3 copy-done.12
  119.5 1.3 copy-done.26
  123.2 1.2 copy-done.68
  125.7 2.9 chain.15
  130.5 1.7 copy-done.6
  132.3 1.3 copy-done.13
  133.6 1.3 copy-done.28
  139.8 3.1 chain.16
  144.8 1.3 copy-done.14
  146.1 1.3 copy-done.30
  152.3 2.9 chain.17
  157.1 1.3 copy-done.15
  158.4 1.3 copy-done.32
  164.6 2.9 chain.18
  169.4 1.3 copy-done.16
  170.8 1.3 copy-done.34
  177.0 2.9 chain.19
  181.8 1.3 copy-done.17
  183.1 1.3 copy-done.36
  189.3 3.1 chain.20
  194.3 1.3 copy-done.18
  195.7 1.3 copy-done.38
  201.9 3.1 chain.21
  204.9 2.3 multiply_reduce_fusion.2
  208.0 2.3 multiply_reduce_fusion.3
  211.0 2.3 multiply_reduce_fusion.1
  214.1 2.3 multiply_reduce_fusion
  216.4 1.3 collective-permute-start.29
  219.7 1.3 collective-permute-start.33
  221.0 155.4 %collective-permute-done.33 = f32[2,1024]{1,0:T(2,128)S(1)} collective-permute-done((f32[2,1024]{1,0:T(2,128)S(1)}, f32[2,1024]{1,0:T(2,128)S(1)}, u32[]{:S(2)}, u32[]{:S(2)}) %collective-permute-start.33) | collective-permute-done | bytes 8224 | tf_op jit(solution)/shard_map/ppermute | solution.py:114
  377.1 1.2 add_bitcast_fusion
  (240 shorter events, 76.1 us)
Async XLA Ops:
  0.6 1.7 copy-start
  2.7 3.6 collective-permute-start
  3.4 3.6 collective-permute-start.1
  4.0 27.9 %collective-permute-start.4 = (bf16[256,2048]{1,0:T(8,128)(2,1)}, bf16[256,2048]{1,0:T(8,128)(2,1)S(1)}, u32[]{:S(2)}, u32[]{:S(2)}) collective-permute-start(bf16[256,2048]{1,0:T(8,128)(2,1)} %bitcast.5), channel_id=1, source_target_pairs={{0,2},{4,5},{8,9},{12,14},{16,18},{20,21},{24,25},{28,30}} | collective-permute-start | bytes 3145736 | tf_op jit(solution)/shard_map/ppermute | solution.py:111
  4.8 38.2 %collective-permute-start.5 = (bf16[256,2048]{1,0:T(8,128)(2,1)}, bf16[256,2048]{1,0:T(8,128)(2,1)S(1)}, u32[]{:S(2)}, u32[]{:S(2)}) collective-permute-start(bf16[256,2048]{1,0:T(8,128)(2,1)} %bitcast.5), channel_id=1, source_target_pairs={{1,2},{5,5},{9,9},{13,14},{17,18},{21,21},{25,25},{29,30}} | collective-permute-start | bytes 3145736 | tf_op jit(solution)/shard_map/ppermute | solution.py:111
  5.5 40.1 %collective-permute-start.6 = (bf16[256,2048]{1,0:T(8,128)(2,1)}, bf16[256,2048]{1,0:T(8,128)(2,1)S(1)}, u32[]{:S(2)}, u32[]{:S(2)}) collective-permute-start(bf16[256,2048]{1,0:T(8,128)(2,1)} %bitcast.5), channel_id=1, source_target_pairs={{2,2},{6,5},{10,9},{14,14},{18,18},{22,21},{26,25},{30,30}} | collective-permute-start | bytes 3145736 | tf_op jit(solution)/shard_map/ppermute | solution.py:111
  6.3 14.2 %collective-permute-start.2 = (bf16[160,1024]{1,0:T(8,128)(2,1)S(1)}, bf16[160,1024]{1,0:T(8,128)(2,1)S(1)}, u32[]{:S(2)}, u32[]{:S(2)}) collective-permute-start(bf16[160,1024]{1,0:T(8,128)(2,1)S(1)} %convolution_convert_fusion.1), channel_id=1, source_target_pairs={{2,2},{6,5},{10,9},{14,14},{18,18},{22,21},{26,25},{30,30}} | collective-permute-start | bytes 983048 | tf_op jit(solution)/shard_map/ppermute | solution.py:111
  7.0 16.8 %collective-permute-start.3 = (bf16[160,1024]{1,0:T(8,128)(2,1)S(1)}, bf16[160,1024]{1,0:T(8,128)(2,1)S(1)}, u32[]{:S(2)}, u32[]{:S(2)}) collective-permute-start(bf16[160,1024]{1,0:T(8,128)(2,1)S(1)} %convolution_convert_fusion.1), channel_id=1, source_target_pairs={{3,2},{7,5},{11,9},{15,14},{19,18},{23,21},{27,25},{31,30}} | collective-permute-start | bytes 983048 | tf_op jit(solution)/shard_map/ppermute | solution.py:111
  20.5 5.3 %copy-start.91 = (bf16[160,1024]{1,0:T(8,128)(2,1)}, bf16[160,1024]{1,0:T(8,128)(2,1)S(1)}, u32[]{:S(2)}) copy-start(bf16[160,1024]{1,0:T(8,128)(2,1)S(1)} %collective-permute-done.2) | copy-start | bytes 983044
  20.5 3.9 %collective-permute-start.12 = (bf16[160,1024]{1,0:T(8,128)(2,1)S(1)}, bf16[160,1024]{1,0:T(8,128)(2,1)S(1)}, u32[]{:S(2)}, u32[]{:S(2)}) collective-permute-start(bf16[160,1024]{1,0:T(8,128)(2,1)S(1)} %convolution_convert_fusion), channel_id=1, source_target_pairs={{28,30}} | collective-permute-start | bytes 983048 | tf_op jit(solution)/shard_map/ppermute | solution.py:111
  23.7 2.1 copy-start.93
  23.7 1.4 collective-permute-start.13
  24.4 1.4 collective-permute-start.14
  25.1 5.2 %collective-permute-start.15 = (bf16[160,1024]{1,0:T(8,128)(2,1)S(1)}, bf16[160,1024]{1,0:T(8,128)(2,1)S(1)}, u32[]{:S(2)}, u32[]{:S(2)}) collective-permute-start(bf16[160,1024]{1,0:T(8,128)(2,1)S(1)} %convolution_convert_fusion), channel_id=1, source_target_pairs={{31,30}} | collective-permute-start | bytes 983048 | tf_op jit(solution)/shard_map/ppermute | solution.py:111
  25.8 23.9 %collective-permute-start.7 = (bf16[256,2048]{1,0:T(8,128)(2,1)}, bf16[256,2048]{1,0:T(8,128)(2,1)S(1)}, u32[]{:S(2)}, u32[]{:S(2)}) collective-permute-start(bf16[256,2048]{1,0:T(8,128)(2,1)} %bitcast.5), channel_id=1, source_target_pairs={{3,2},{7,5},{11,9},{15,14},{19,18},{23,21},{27,25},{31,30}} | collective-permute-start | bytes 3145736 | tf_op jit(solution)/shard_map/ppermute | solution.py:111
  30.3 30.9 %collective-permute-start.10 = (bf16[512,1024]{1,0:T(8,128)(2,1)}, bf16[512,1024]{1,0:T(8,128)(2,1)}, u32[]{:S(2)}, u32[]{:S(2)}) collective-permute-start(bf16[512,1024]{1,0:T(8,128)(2,1)} %bitcast.29), channel_id=1, source_target_pairs={{2,2},{6,5},{10,9},{14,14},{18,18},{22,21},{26,25},{30,30}} | collective-permute-start | bytes 3145736 | tf_op jit(solution)/shard_map/ppermute | solution.py:111
  32.9 39.3 %collective-permute-start.11 = (bf16[512,1024]{1,0:T(8,128)(2,1)}, bf16[512,1024]{1,0:T(8,128)(2,1)}, u32[]{:S(2)}, u32[]{:S(2)}) collective-permute-start(bf16[512,1024]{1,0:T(8,128)(2,1)} %bitcast.29), channel_id=1, source_target_pairs={{3,2},{7,5},{11,9},{15,14},{19,18},{23,21},{27,25},{31,30}} | collective-permute-start | bytes 3145736 | tf_op jit(solution)/shard_map/ppermute | solution.py:111
  43.9 28.3 %collective-permute-start.8 = (bf16[512,1024]{1,0:T(8,128)(2,1)}, bf16[512,1024]{1,0:T(8,128)(2,1)}, u32[]{:S(2)}, u32[]{:S(2)}) collective-permute-start(bf16[512,1024]{1,0:T(8,128)(2,1)} %bitcast.29), channel_id=1, source_target_pairs={{0,2},{4,5},{8,9},{12,14},{16,18},{20,21},{24,25},{28,30}} | collective-permute-start | bytes 3145736 | tf_op jit(solution)/shard_map/ppermute | solution.py:111
  46.6 25.6 %collective-permute-start.9 = (bf16[512,1024]{1,0:T(8,128)(2,1)}, bf16[512,1024]{1,0:T(8,128)(2,1)}, u32[]{:S(2)}, u32[]{:S(2)}) collective-permute-start(bf16[512,1024]{1,0:T(8,128)(2,1)} %bitcast.29), channel_id=1, source_target_pairs={{1,2},{5,5},{9,9},{13,14},{17,18},{21,21},{25,25},{29,30}} | collective-permute-start | bytes 3145736 | tf_op jit(solution)/shard_map/ppermute | solution.py:111
  49.3 1.9 copy-start.64
  49.4 22.9 %copy-start.8 = (bf16[640,1024]{1,0:T(8,128)(2,1)}, bf16[640,1024]{1,0:T(8,128)(2,1)S(1)}, u32[]{:S(2)}) copy-start(bf16[640,1024]{1,0:T(8,128)(2,1)S(1)} %constant_dynamic-update-slice_fusion.x_ref) | copy-start | bytes 3932164
  49.4 2.4 copy-start.40
  49.4 2.7 copy-start.52
  49.4 2.6 copy-start.87
  53.3 19.0 %copy-start.88 = (f32[1,1024]{1,0:T(1,128)S(1)}, f32[1,1024]{1,0:T(1,128)}, u32[]{:S(2)}) copy-start(f32[1,1024]{1,0:T(1,128)} %scale_ref.21) | copy-start | bytes 12292
  59.7 1.5 copy-start.89
  61.2 14.0 %copy-start.1 = (bf16[640,2048]{1,0:T(8,128)(2,1)}, bf16[640,2048]{1,0:T(8,128)(2,1)S(1)}, u32[]{:S(2)}) copy-start(bf16[640,2048]{1,0:T(8,128)(2,1)S(1)} %get-tuple-element.38.slope_ref) | copy-start | bytes 7864324
  76.3 0.8 collective-permute-start.16
  77.1 1.7 copy-start.2
  80.2 1.3 copy-start.20
  86.4 5.0 %copy-start.3 = (bf16[640,2048]{1,0:T(8,128)(2,1)S(1)}, bf16[640,2048]{1,0:T(8,128)(2,1)}, u32[]{:S(2)}) copy-start(bf16[640,2048]{1,0:T(8,128)(2,1)} %copy-done.1) | copy-start | bytes 7864324
  90.6 0.8 collective-permute-start.17
  91.3 1.3 copy-start.10
  102.9 0.8 collective-permute-start.18
  103.7 1.7 copy-start.4
  105.5 1.3 copy-start.11
  106.8 1.3 copy-start.24
  113.0 5.2 %copy-start.5 = (bf16[640,2048]{1,0:T(8,128)(2,1)S(1)}, bf16[640,2048]{1,0:T(8,128)(2,1)}, u32[]{:S(2)}) copy-start(bf16[640,2048]{1,0:T(8,128)(2,1)} %copy-done.1) | copy-start | bytes 7864324
  117.4 0.8 collective-permute-start.19
  118.1 1.3 copy-start.12
  119.5 1.3 copy-start.26
  129.7 0.8 collective-permute-start.20
  130.5 1.7 copy-start.6
  133.6 1.3 copy-start.28
  139.8 5.0 %copy-start.7 = (bf16[640,2048]{1,0:T(8,128)(2,1)S(1)}, bf16[640,2048]{1,0:T(8,128)(2,1)}, u32[]{:S(2)}) copy-start(bf16[640,2048]{1,0:T(8,128)(2,1)} %copy-done.1) | copy-start | bytes 7864324
  144.0 0.8 collective-permute-start.21
  144.8 1.3 copy-start.14
  156.3 0.8 collective-permute-start.22
  157.1 1.3 copy-start.15
  168.7 0.8 collective-permute-start.23
  169.4 1.3 copy-start.16
  181.0 0.8 collective-permute-start.24
  181.8 1.3 copy-start.17
  193.6 0.8 collective-permute-start.25
  194.3 1.3 copy-start.18
  201.9 3.1 copy-start.90
  207.3 169.8 %collective-permute-start.27 = (bf16[512,1024]{1,0:T(8,128)(2,1)S(1)}, bf16[512,1024]{1,0:T(8,128)(2,1)S(1)}, u32[]{:S(2)}, u32[]{:S(2)}) collective-permute-start(bf16[512,1024]{1,0:T(8,128)(2,1)S(1)} %get-tuple-element.72), channel_id=1, source_target_pairs={{2,1},{5,5},{9,9},{14,13},{18,17},{21,21},{25,25},{30,29}} | collective-permute-start | bytes 3145736 | tf_op jit(solution)/shard_map/ppermute | solution.py:114
  210.3 166.8 %collective-permute-start.26 = (bf16[512,1024]{1,0:T(8,128)(2,1)S(1)}, bf16[512,1024]{1,0:T(8,128)(2,1)S(1)}, u32[]{:S(2)}, u32[]{:S(2)}) collective-permute-start(bf16[512,1024]{1,0:T(8,128)(2,1)S(1)} %get-tuple-element.74), channel_id=1, source_target_pairs={{2,0},{5,4},{9,8},{14,12},{18,16},{21,20},{25,24},{30,28}} | collective-permute-start | bytes 3145736 | tf_op jit(solution)/shard_map/ppermute | solution.py:114
  213.3 163.8 %collective-permute-start.28 = (bf16[512,1024]{1,0:T(8,128)(2,1)S(1)}, bf16[512,1024]{1,0:T(8,128)(2,1)S(1)}, u32[]{:S(2)}, u32[]{:S(2)}) collective-permute-start(bf16[512,1024]{1,0:T(8,128)(2,1)S(1)} %get-tuple-element.76), channel_id=1, source_target_pairs={{2,2},{5,6},{9,10},{14,14},{18,18},{21,22},{25,26},{30,30}} | collective-permute-start | bytes 3145736 | tf_op jit(solution)/shard_map/ppermute | solution.py:114
  216.4 160.7 %collective-permute-start.29 = (bf16[512,1024]{1,0:T(8,128)(2,1)S(1)}, bf16[512,1024]{1,0:T(8,128)(2,1)S(1)}, u32[]{:S(2)}, u32[]{:S(2)}) collective-permute-start(bf16[512,1024]{1,0:T(8,128)(2,1)S(1)} %get-tuple-element.78), channel_id=1, source_target_pairs={{2,3},{5,7},{9,11},{14,15},{18,19},{21,23},{25,27},{30,31}} | collective-permute-start | bytes 3145736 | tf_op jit(solution)/shard_map/ppermute | solution.py:114
  217.7 0.7 collective-permute-start.30
  218.4 0.7 collective-permute-start.31
  219.1 0.7 collective-permute-start.32
  219.7 156.7 %collective-permute-start.33 = (f32[2,1024]{1,0:T(2,128)S(1)}, f32[2,1024]{1,0:T(2,128)S(1)}, u32[]{:S(2)}, u32[]{:S(2)}) collective-permute-start(f32[2,1024]{1,0:T(2,128)S(1)} %pad_maximum_fusion.1), channel_id=1, source_target_pairs={{2,3},{5,7},{9,11},{14,15},{18,19},{21,23},{25,27},{30,31}} | collective-permute-start | bytes 24584 | tf_op jit(solution)/shard_map/ppermute | solution.py:114
  (65 other events, 78.0 us)
